TPU v7x, 256 devices: a whole 4x4x8 slice. The times are simulated.
256 devices in a mesh: space: 8 (over x_hi, y), tm: 32 (over x_lo, z, core).
Axes of the slice: x: 4 (x_hi: 2, x_lo: 2; x = x_hi * 2 + x_lo), y: 4, z: 8, core: 2. Of those that a mesh axis runs over, the one named last changes fastest.
Arguments:
- fields: float32 [16384, 32768], P('space', 'tm'), may hold values from -6 to 6
- range_test: float32 [32768, 64], P('tm'), may hold values from -0.03125 to 0.03125
- corange_test: float32 [128, 16384], P(None, 'space'), may hold values from -0.0625 to 0.0625
- core_left: float32 [256, 16384], P(None, 'space'), may hold values from -0.0625 to 0.0625
- core_right: float32 [256, 32768], P(None, 'tm'), may hold values from -0.0625 to 0.0625
Outputs:
- range_sketch: float32 [16384, 64], P('space')
- corange_sketch: float32 [128, 32768], P('space', 'tm')
- core_sketch: float32 [256, 256], P('space', 'tm')
All inputs are finite; a program needn't handle non-finite values.
Results may differ from a plain program's by a relative error of at most 0.000073.
Values sent between devices are 32-bit elements; how exact they have to be, the bound alone decides.
A program may use at most 64 MiB of HBM per device.

v0:
```python
import jax
import jax.numpy as jnp
from jax import lax
from jax.sharding import PartitionSpec as P


def shards(fields, range_test, corange_test, core_left, core_right):
    highest = lax.Precision.HIGHEST
    partial_range = jnp.dot(
        fields, range_test, precision=highest, preferred_element_type=jnp.float32
    )
    range_sketch = lax.psum(partial_range, "tm")
    space_count = lax.axis_size("space")
    time_count = lax.axis_size("tm")
    corange_sketch = lax.psum_scatter(
        jnp.dot(corange_test, fields, precision=highest, preferred_element_type=jnp.float32),
        "space",
        scatter_dimension=0,
        tiled=True,
    )
    core_order = core_left.shape[0]
    row_count = core_order // space_count
    col_count = core_order // time_count
    mixed = jnp.dot(core_left, fields, precision=highest, preferred_element_type=jnp.float32)
    local_core = jnp.einsum(
        "sc,tc->st", mixed, core_right, precision=highest, preferred_element_type=jnp.float32
    )
    tiled = local_core.reshape(space_count, row_count, time_count, col_count)
    tiled = jnp.transpose(tiled, (0, 2, 1, 3)).reshape(
        space_count * time_count * row_count, col_count
    )
    core_sketch = lax.psum_scatter(tiled, ("space", "tm"), scatter_dimension=0, tiled=True)
    return (range_sketch, corange_sketch, core_sketch)


def solution(mesh):
    placed = (P("space", "tm"), P("tm", None), P(None, "space"), P(None, "space"), P(None, "tm"))
    return jax.shard_map(
        shards,
        mesh=mesh,
        in_specs=placed,
        out_specs=(P("space", None), P("space", "tm"), P("space", "tm")),
        check_vma=False,
    )
```

profile of v0, /device:TPU:1, one launch (start us, length us, event | category | flops | bytes accessed | tf_op | source)
XLA Modules:
  0.0 1380.5 jit_solution(3148288469750223722)
XLA Ops:
  8.0 0.0 copy-start
  8.0 0.0 copy-start.2
  8.0 0.0 reduce-scatter.7.cloned.1.call-start
  8.1 1.5 copy-done
  9.6 9.8 fusion.2
  19.4 0.0 copy-done.2
  19.4 1.0 fusion.3
  20.4 0.3 reshape.12
  20.7 0.0 copy-start.3
  20.7 2.7 copy.17
  23.4 0.0 copy-start.1
  23.4 0.0 reduce-scatter.7.cloned.1.call-update
  23.5 0.0 all-reduce.2.cloned.1.call-start
  23.5 0.0 copy-done.3
  23.5 11.4 fusion
  34.9 0.0 all-reduce.2.cloned.1.call-update
  34.9 0.0 reduce-scatter.5.cloned.1.call-start
  35.0 0.0 copy-done.1
  35.0 7.8 fusion.1
  42.8 0.0 reduce-scatter.5.cloned.1.call-update
  42.8 1252.4 %reduce-scatter.7.cloned.1.call-done = f32[32,8]{1,0:T(8,128)} async-done(((f32[8192,8]{1,0:T(8,128)}), f32[32,8]{1,0:T(8,128)}) %reduce-scatter.7.cloned.1.call-update) | async-done | bytes 1040
  1295.3 1.4 copy.16
  1296.7 0.0 all-reduce.2.cloned.1.call-done
  1296.7 74.5 %reduce-scatter.5.cloned.1.call-done = f32[16,1024]{1,0:T(8,128)} async-done(((f32[128,1024]{1,0:T(8,128)}), f32[16,1024]{1,0:T(8,128)}) %reduce-scatter.5.cloned.1.call-update) | async-done | bytes 65552 | tf_op jit(solution)/shard_map/reduce_scatter | solution.py:15
  1371.2 1.9 copy.20
Async XLA Ops:
  8.0 1.6 copy-start
  8.0 11.4 copy-start.2
  8.0 1287.3 %reduce-scatter.7.cloned.1.call-start = ((), (), s32[]{:S(2)}) async-start(), calls=%async_computation.4 | async-start | bytes 4210688
  20.7 2.8 copy-start.3
  23.4 11.6 copy-start.1
  23.5 1273.2 %all-reduce.2.cloned.1.call-start = ((), (), s32[]{:S(2)}) async-start(), calls=%async_computation.2 | async-start | bytes 1048576 | tf_op jit(solution)/shard_map/psum | solution.py:12
  34.9 1336.2 %reduce-scatter.5.cloned.1.call-start = ((), (), s32[]{:S(2)}) async-start(), calls=%async_computation.3 | async-start | bytes 589824 | tf_op jit(solution)/shard_map/reduce_scatter | solution.py:15
Sparse Core Ops, SparseCore 0:
  23.6 1271.6 reduce-scatter.6
  1299.7 71.4 reduce-scatter.4
Sparse Core Ops, SparseCore 1:
  35.0 226.1 all-reduce.1
where the time goes:
time: 1380 us
  waiting for transfers between devices  1330 us (96%)
  matrix products  30 us (2%)
  between operations  15.5 us (1%)
    unnamed x4, waiting for transfers between devices  1250 us
    reduce_scatter x1, waiting for transfers between devices, shards(): lax.psum_scatter(jnp.dot(corange_test, fields, precision=highest, preferr...  74.5 us
  transfers between devices with their start and end apart: 3, of which 2 were waited for; matrix products, arithmetic and copies ran while one was open for 1% of the time, Pallas kernels for 0%

commit v1 on v0

v1 whole, which is shorter than its diff:
```python
import jax
import jax.numpy as jnp
from jax import lax
from jax.experimental import pallas as pl
from jax.experimental.pallas import tpu as pltpu
from jax.sharding import PartitionSpec as P

MESH = pl.DeviceIdType.MESH
F32, BF16 = jnp.float32, jnp.bfloat16
NN = (((1,), (0,)), ((), ()))
NT = (((1,), (1,)), ((), ()))
XH, Y, XL, Z, C = 2, 4, 2, 8, 2
CHUNK = 512
WIDTH = 512
PLANE = sorted(
    ((i, j, k) for i in range(XH) for j in range(Y) for k in range(XL) if i or j or k),
    key=lambda p: (-2 * p[0] - min(p[1], Y - p[1]) - p[2], p),
)
COLUMN = sorted(
    ((i, j) for i in range(Z) for j in range(C) if i or j), key=lambda p: (-min(p[0], Z - p[0]), p)
)
ROUND = sorted(
    ((i, k) for i in range(Z) for k in range(XL) if i or k), key=lambda p: (-min(p[0], Z - p[0]) - p[1], p)
)
RING = (2, 1, 3)


def dot(a, b, dims):
    return lax.dot_general(a, b, dims, preferred_element_type=F32)


def split(x):
    high = x.astype(BF16)
    return high, (x - high.astype(F32)).astype(BF16)


def kernel(
    f_hbm, r_hbm, a_hbm, l_hbm, q_hbm,
    range_ref, corange_ref, core_ref,
    f, r, a, l, q, fh, fl, rr, al, qh, ql, mh, ml,
    rp, rc, rz, cp, cy, cs, cx, mp, ma, mb, mc,
    load_f, load, core_s, core_r, z_s, z_r, ag_s, ag_r, xg_s, xg_r, cg_s, cg_r,
    cy_s, cy_r, cx_s, cx_r, ma_s, ma_r, mb_s, mb_r,
):
    s, t = lax.axis_index("space"), lax.axis_index("tm")
    xh, y = s // Y, s % Y
    xl, z, c = t // (Z * C), (t // C) % Z, t % C

    def at(dxh=0, dy=0, dxl=0, dz=0, dc=0):
        return (
            lax.rem(xh + dxh, XH) * Y + lax.rem(y + dy, Y),
            lax.rem(xl + dxl, XL) * (Z * C) + lax.rem(z + dz, Z) * C + lax.rem(c + dc, C),
        )

    def remote(src, dst, ss, rs_, **where):
        return pltpu.make_async_remote_copy(
            src_ref=src, dst_ref=dst, send_sem=ss, recv_sem=rs_, device_id=at(**where), device_id_type=MESH
        )

    def whole(ref, ss, rs_):
        return remote(ref, ref, ss, rs_, dc=1)

    n_chunks = f.shape[0]
    half = n_chunks // C
    groups = CHUNK // 128
    other = lax.rem(c + 1, C)
    xo = lax.rem(xl + 1, XL)

    loads = [
        pltpu.make_async_copy(src, dst, load.at[i])
        for i, (src, dst) in enumerate(((r_hbm, r), (l_hbm, l), (a_hbm, a), (q_hbm, q)))
    ]

    def f_load(chunk):
        rows = pl.ds(pl.multiple_of(chunk * CHUNK, CHUNK), CHUNK)
        return pltpu.make_async_copy(f_hbm.at[rows, :], f.at[chunk], load_f.at[chunk])

    loads[0].start()
    for k in range(half):
        f_load(other * half + k).start()
    for k in range(half):
        f_load(c * half + k).start()
    for cp_ in loads[1:]:
        cp_.start()

    barrier = pltpu.get_barrier_semaphore()
    peers = {(i, j, k, 0, 0) for i, j, k in PLANE} | {(0, 0, 0, i, j) for i, j in COLUMN}
    peers |= {(0, 0, k, i, 0) for i, k in ROUND}

    def far(p):
        return -(2 * p[0] + min(p[1], Y - p[1]) + p[2] + min(p[3], Z - p[3])), p

    for i, j, k, m, n in sorted(peers, key=far):
        pl.semaphore_signal(
            barrier, inc=1, device_id=at(dxh=i, dy=j, dxl=k, dz=m, dc=n), device_id_type=MESH
        )

    loads[0].wait()
    high, low = split(r[...])
    kk = high.shape[0]
    rr[:kk, :] = high
    rr[kk:, :] = low

    def range_chunk(chunk):
        f_load(chunk).wait()
        high, low = split(f[chunk])
        rows = pl.ds(pl.multiple_of(chunk * CHUNK, CHUNK), CHUNK)
        for j in range(fh.shape[0]):
            fh[j, rows, :] = high[:, j * WIDTH : (j + 1) * WIDTH]
            fl[j, rows, :] = low[:, j * WIDTH : (j + 1) * WIDTH]
        both = dot(rr[...], high, NT)
        out = both[:kk] + both[kk:] + dot(rr[:kk, :], low, NT)
        for i in range(groups):
            rp[groups * chunk + i] = out[:, 128 * i : 128 * (i + 1)]

    def core_copy(k):
        return remote(
            rp.at[pl.ds(other * Z + groups * k, groups)], rc.at[pl.ds(groups * k, groups)],
            core_s, core_r, dc=1,
        )

    @pl.loop(0, n_chunks - 1)
    def _(k):
        range_chunk(lax.rem(other * half + k, n_chunks))

    pl.semaphore_wait(barrier, len(peers))
    for k in range(half):
        core_copy(k).start()
    range_chunk(c * half + half - 1)

    krows = kk // XL
    mine = pl.ds(pl.multiple_of(xl * krows, krows), krows)
    theirs = pl.ds(pl.multiple_of(xo * krows, krows), krows)

    whole(rc, core_s, core_r).wait_recv()
    for i in range(Z):
        rp[c * Z + i] = rp[c * Z + i] + rc[i]

    def z_copy(n):
        i, k = ROUND[n]
        rows_ = theirs if k else mine
        return remote(rp.at[c * Z + lax.rem(z + i, Z), rows_], rz.at[n], z_s, z_r, dz=i, dxl=k)

    for n in range(len(ROUND)):
        z_copy(n).start()

    loads[1].wait()
    loads[2].wait()
    c_rows, m_rows = a.shape[0], l.shape[0]
    rows = c_rows + m_rows
    high, low = split(a[...])
    al[:c_rows, :] = high
    al[rows : rows + c_rows, :] = low
    high, low = split(l[...])
    al[c_rows:rows, :] = high
    al[rows + c_rows :, :] = low
    loads[3].wait()
    high, low = split(q[...])
    qh[...] = high
    ql[...] = low

    piece = c_rows // (XH * Y)

    def cy_copy(dy, j):
        return remote(cp.at[j, lax.rem(y + dy, Y)], cy.at[j, dy - 1], cy_s, cy_r.at[j], dy=dy)

    def cx_copy(j):
        return remote(cs.at[j, lax.rem(xh + 1, XH)], cx.at[j], cx_s.at[j], cx_r.at[j], dxh=1)

    n_cols = fh.shape[0]

    @pl.loop(0, n_cols)
    def _(j):
        both = dot(al[...], fh[j], NN)
        out = both[:rows] + both[rows:] + dot(al[:rows, :], fl[j], NN)
        for i in range(XH):
            for k in range(Y):
                n = i * Y + k
                cp[j, k, i] = out[n * piece : (n + 1) * piece]
        high, low = split(out[c_rows:])
        mh[j] = high
        ml[j] = low
        for dy in RING:
            cy_copy(dy, j).start()

    total = None
    for j in range(n_cols):
        cols = slice(j * WIDTH, (j + 1) * WIDTH)
        part = dot(mh[j], qh[:, cols], NT) + dot(ml[j], qh[:, cols], NT) + dot(mh[j], ql[:, cols], NT)
        total = part if total is None else total + part

    trows = m_rows // (XH * Y)
    for i in range(XH * Y):
        for k in range(XL):
            mp[i, k] = total[i * trows : (i + 1) * trows, k * 128 : (k + 1) * 128]

    def ma_copy(n):
        i, j, k = PLANE[n]
        to = lax.rem(xh + i, XH) * Y + lax.rem(y + j, Y)
        return remote(mp.at[to, lax.rem(xl + k, XL)], ma.at[n], ma_s, ma_r, dxh=i, dy=j, dxl=k)

    for n in range(len(PLANE)):
        ma_copy(n).start()

    def pass_on(j):
        whole(cy.at[j], cy_s, cy_r.at[j]).wait_recv()
        cs[j] = cp[j, y] + cy[j, 0] + cy[j, 1] + cy[j, 2]
        cx_copy(j).start()

    for j in range(n_cols - 1):
        pass_on(j)

    whole(rz, z_s, z_r).wait_recv()
    done = rp[c * Z + z, mine]
    for n in range(len(ROUND)):
        done = done + rz[n]

    def spot(cc, zz, rows_):
        return range_ref.at[rows_, pl.ds(pl.multiple_of((cc * Z + zz) * 128, 128), 128)]

    own_piece = spot(c, z, mine)
    own_piece[...] = done

    def ag_copy(d):
        return remote(own_piece, own_piece, ag_s, ag_r.at[d - 1], dz=d)

    def ag_arrival(d):
        there = spot(c, lax.rem(z + Z - d, Z), mine)
        return remote(there, there, ag_s, ag_r.at[d - 1], dz=d)

    def xg_copy(d):
        there = spot(c, lax.rem(z + Z - d, Z), mine)
        return remote(there, there, xg_s, xg_r.at[d], dxl=1)

    def xg_arrival(d):
        there = spot(c, lax.rem(z + Z - d, Z), theirs)
        return remote(there, there, xg_s, xg_r.at[d], dxl=1)

    def cg_copy(d, k):
        there = spot(c, lax.rem(z + Z - d, Z), (mine, theirs)[k])
        return remote(there, there, cg_s, cg_r, dc=1)

    for d in (4, 3, 5, 2, 6, 1, 7):
        ag_copy(d).start()
    xg_copy(0).start()
    cg_copy(0, 0).start()

    def forward(order):
        for d in order:
            ag_arrival(d).wait_recv()
            xg_copy(d).start()
            cg_copy(d, 0).start()

    pass_on(n_cols - 1)

    whole(ma, ma_s, ma_r).wait_recv()
    part = mp[s, xl]
    for n in range(len(PLANE)):
        part = part + ma[n]
    part = jnp.concatenate([part, jnp.zeros((128 - trows, 128), F32)], 0).T
    for i in range(Z * C):
        mb[i] = part[8 * i : 8 * i + 8]

    def mb_copy(n):
        i, j = COLUMN[n]
        to = lax.rem(z + i, Z) * C + lax.rem(c + j, C)
        return remote(mb.at[to], mc.at[n], mb_s, mb_r, dz=i, dc=j)

    for n in range(len(COLUMN)):
        mb_copy(n).start()

    forward((1, 7, 2, 6, 3, 5, 4))
    arrivals = (0, 1, 7, 2, 6, 3, 5, 4)
    for d in arrivals:
        xg_arrival(d).wait_recv()
        cg_copy(d, 1).start()

    for j in range(n_cols):
        cx_copy(j).wait_recv()
        corange_ref[:, j * WIDTH : (j + 1) * WIDTH] = cs[j, xh] + cx[j]

    whole(mc, mb_s, mb_r).wait_recv()
    out = mb[z * C + c]
    for n in range(len(COLUMN)):
        out = out + mc[n]
    core_ref[...] = out[:, :trows]

    whole(rc, cg_s, cg_r).wait_recv()

    whole(rc, core_s, core_r).wait_send()
    whole(rz, z_s, z_r).wait_send()
    whole(rz.at[pl.ds(0, Z - 1)], ag_s, ag_r.at[0]).wait_send()
    whole(rc.at[:, mine], xg_s, xg_r.at[0]).wait_send()
    whole(rc, cg_s, cg_r).wait_send()
    whole(ma, ma_s, ma_r).wait_send()
    whole(mc, mb_s, mb_r).wait_send()
    whole(cy, cy_s, cy_r.at[0]).wait_send()
    for j in range(n_cols):
        cx_copy(j).wait_send()


def store(*refs):
    half = len(refs) // 2
    sems = refs[-1]
    copies = [pltpu.make_async_copy(refs[i], refs[half + i], sems.at[i]) for i in range(half)]
    for copy in copies:
        copy.start()
    for copy in copies:
        copy.wait()


def shards(fields, range_test, corange_test, core_left, core_right):
    cells, snaps = fields.shape
    k, l, m = range_test.shape[1], corange_test.shape[0], core_left.shape[0]
    n_cols = snaps // WIDTH
    vmem = pl.BlockSpec(memory_space=pltpu.VMEM)
    hbm = pl.BlockSpec(memory_space=pltpu.HBM)
    dma = pltpu.SemaphoreType.DMA
    v = pltpu.VMEM
    outs = (
        jax.ShapeDtypeStruct((k, cells), F32),
        jax.ShapeDtypeStruct((l // (XH * Y), snaps), F32),
        jax.ShapeDtypeStruct((m // (XL * Z * C), m // (XH * Y)), F32),
    )
    results = pl.pallas_call(
        kernel,
        out_shape=outs,
        in_specs=[hbm] * 5,
        out_specs=(vmem,) * 3,
        scratch_shapes=[
            v((cells // CHUNK, CHUNK, snaps), F32),
            v((k, snaps), F32),
            v((l, cells), F32),
            v((m, cells), F32),
            v((m, snaps), F32),
            v((n_cols, cells, WIDTH), BF16),
            v((n_cols, cells, WIDTH), BF16),
            v((2 * k, snaps), BF16),
            v((2 * (l + m), cells), BF16),
            v((m, snaps), BF16),
            v((m, snaps), BF16),
            v((n_cols, m, WIDTH), BF16),
            v((n_cols, m, WIDTH), BF16),
            v((Z * C, k, 128), F32),
            v((Z, k, 128), F32),
            v((len(ROUND), k // XL, 128), F32),
            v((n_cols, Y, XH, l // (XH * Y), WIDTH), F32),
            v((n_cols, Y - 1, XH, l // (XH * Y), WIDTH), F32),
            v((n_cols, XH, l // (XH * Y), WIDTH), F32),
            v((n_cols, l // (XH * Y), WIDTH), F32),
            v((XH * Y, XL, m // (XH * Y), 128), F32),
            v((len(PLANE), m // (XH * Y), 128), F32),
            v((Z * C, 8, 128), F32),
            v((len(COLUMN), 8, 128), F32),
            dma((cells // CHUNK,)),
            dma((4,)),
            dma, dma,
            dma, dma,
            dma, dma((Z - 1,)),
            dma, dma((Z,)),
            dma, dma,
            dma, dma((n_cols,)),
            dma((n_cols,)), dma((n_cols,)),
            dma, dma,
            dma, dma,
        ],
        compiler_params=pltpu.CompilerParams(
            collective_id=0, has_side_effects=True, vmem_limit_bytes=48 << 20
        ),
        name="sketch",
    )(*(
        pltpu.with_memory_space_constraint(x, pltpu.HBM)
        for x in (fields, range_test.T, corange_test, core_left, core_right)
    ))
    range_t, corange, core_t = pl.pallas_call(
        store,
        out_shape=outs,
        in_specs=[pl.BlockSpec(memory_space=pl.ANY)] * 3,
        out_specs=(hbm,) * 3,
        scratch_shapes=[dma((3,))],
        name="store",
    )(*(pltpu.with_memory_space_constraint(x, pltpu.VMEM) for x in results))
    return range_t.T, corange, core_t.T


def solution(mesh):
    placed = (P("space", "tm"), P("tm", None), P(None, "space"), P(None, "space"), P(None, "tm"))
    return jax.shard_map(
        shards,
        mesh=mesh,
        in_specs=placed,
        out_specs=(P("space", None), P("space", "tm"), P("space", "tm")),
        check_vma=False,
    )
```

time: 1380 us -> 34.5 us (0.03)
  waiting for transfers between devices: 1330 us -> 0 us
  Pallas kernels: 0 us -> 33.8 us
  matrix products: 30 us -> 0 us
  between operations: 15.5 us -> 0.64 us
    unnamed x4 -> x0, waiting for transfers between devices: 1250 us -> none
    reduce_scatter x1 -> x0, waiting for transfers between devices: 74.5 us -> none  [shards(): lax.psum_scatter(jnp.dot(corange_test, fields, precision=highest, preferr...]
    pallas_call x0 -> x2, Pallas kernels: none -> 33.8 us  [the longest x1 32.9 us: shards(): pl.pallas_call(kernel, out_shape=outs, in_specs=[hbm] * 5, out_specs=(vme...]
    dot_general x4 -> x0, matrix products: 30 us -> none  [the longest x1 11.4 us: shards(): jnp.dot(fields, range_test, precision=highest, preferred_element_type=jnp...]
  transfers between devices with their start and end apart: 3 -> 0, of which waited for: 2 -> 0; matrix products, arithmetic and copies ran while one was open for 1% -> 0% of each run, Pallas kernels for 0% -> 0%
where the time goes in v1:
time: 34.5 us; the launch traced here: 34.4 us
  Pallas kernels  33.8 us (98%)
  between operations  0.64 us (2%)
    pallas_call x1, Pallas kernels, shards(): pl.pallas_call(kernel, out_shape=outs, in_specs=[hbm] * 5, out_specs=(vme...  32.9 us
    pallas_call x1, Pallas kernels, shards(): pl.pallas_call(store, out_shape=outs, in_specs=[pl.BlockSpec(memory_space...  0.83 us

profile of v1, /device:TPU:1, one launch (start us, length us, event | category | flops | bytes accessed | tf_op | source)
XLA Modules:
  0.0 34.4 jit_solution(6937553158223445147)
XLA Ops:
  0.6 32.9 %sketch.1 = (f32[64,2048]{1,0:T(8,128)S(1)}, f32[16,1024]{1,0:T(8,128)S(1)}, f32[8,32]{1,0:T(8,128)S(1)}) custom-call(f32[2048,1024]{1,0:T(8,128)} %f_hbm.1, f32[64,1024]{1,0:T(8,128)} %bitcast.3, f32[128,2048]{1,0:T(8,128)} %a_hbm.1, f32[256,2048]{1,0:T(8,128)} %l_hbm.1, f32[256,1024]{1,0:T(8,128)} %q_hbm.1), custom_call_target="tpu_custom_call" | custom-call | tf_op jit(solution)/shard_map/sketch/pallas_call | solution.py:325
  33.6 0.8 %store.1 = (f32[64,2048]{1,0:T(8,128)}, f32[16,1024]{1,0:T(8,128)}, f32[8,32]{1,0:T(8,128)}) custom-call(f32[64,2048]{1,0:T(8,128)S(1)} %get-tuple-element.9.refs_0_, f32[16,1024]{1,0:T(8,128)S(1)} %get-tuple-element.10.refs_1_, f32[8,32]{1,0:T(8,128)S(1)} %get-tuple-element.11.refs_2_), custom_call_target="tpu_custom_call" | custom-call | tf_op jit(solution)/shard_map/store/pallas_call | solution.py:375

commit v2 on v1

--- a/solution.py
+++ b/solution.py
@@ -11,7 +11,7 @@
 NT = (((1,), (1,)), ((), ()))
 XH, Y, XL, Z, C = 2, 4, 2, 8, 2
 CHUNK = 512
-WIDTH = 512
+WIDTH = 256
 PLANE = sorted(
     ((i, j, k) for i in range(XH) for j in range(Y) for k in range(XL) if i or j or k),
     key=lambda p: (-2 * p[0] - min(p[1], Y - p[1]) - p[2], p),
@@ -155,9 +155,6 @@
     al[c_rows:rows, :] = high
     al[rows + c_rows :, :] = low
     loads[3].wait()
-    high, low = split(q[...])
-    qh[...] = high
-    ql[...] = low
 
     piece = c_rows // (XH * Y)
 
@@ -180,8 +177,15 @@
         high, low = split(out[c_rows:])
         mh[j] = high
         ml[j] = low
-        for dy in RING:
-            cy_copy(dy, j).start()
+        cols = pl.ds(pl.multiple_of(j * WIDTH, WIDTH), WIDTH)
+        high, low = split(q[:, cols])
+        qh[:, cols] = high
+        ql[:, cols] = low
+
+        @pl.when(j < n_cols - 1)
+        def _():
+            for dy in RING:
+                cy_copy(dy, j).start()
 
     total = None
     for j in range(n_cols):
@@ -201,14 +205,13 @@
 
     for n in range(len(PLANE)):
         ma_copy(n).start()
+    for dy in RING:
+        cy_copy(dy, n_cols - 1).start()
 
     def pass_on(j):
         whole(cy.at[j], cy_s, cy_r.at[j]).wait_recv()
         cs[j] = cp[j, y] + cy[j, 0] + cy[j, 1] + cy[j, 2]
         cx_copy(j).start()
-
-    for j in range(n_cols - 1):
-        pass_on(j)
 
     whole(rz, z_s, z_r).wait_recv()
     done = rp[c * Z + z, mine]
@@ -251,7 +254,6 @@
             xg_copy(d).start()
             cg_copy(d, 0).start()
 
-    pass_on(n_cols - 1)
 
     whole(ma, ma_s, ma_r).wait_recv()
     part = mp[s, xl]
@@ -269,7 +271,10 @@
     for n in range(len(COLUMN)):
         mb_copy(n).start()
 
-    forward((1, 7, 2, 6, 3, 5, 4))
+    forward((1, 7, 2, 6))
+    for j in range(n_cols):
+        pass_on(j)
+    forward((3, 5, 4))
     arrivals = (0, 1, 7, 2, 6, 3, 5, 4)
     for d in arrivals:
         xg_arrival(d).wait_recv()

time: 34.5 us -> 33.7 us (0.977)
  Pallas kernels: 33.8 us -> 33 us
    pallas_call x1, Pallas kernels: 32.9 us -> 32.2 us  [shards(): pl.pallas_call(kernel, out_shape=outs, in_specs=[hbm] * 5, out_specs=(vme...]
where the time goes in v2:
time: 33.7 us; the launch traced here: 33.6 us
  Pallas kernels  33 us (98%)
  between operations  0.64 us (2%)
    pallas_call x1, Pallas kernels, shards(): pl.pallas_call(kernel, out_shape=outs, in_specs=[hbm] * 5, out_specs=(vme...  32.2 us
    pallas_call x1, Pallas kernels, shards(): pl.pallas_call(store, out_shape=outs, in_specs=[pl.BlockSpec(memory_space...  0.83 us

profile of v2, /device:TPU:1, one launch (start us, length us, event | category | flops | bytes accessed | tf_op | source)
XLA Modules:
  0.0 33.6 jit_solution(15034667164403402574)
XLA Ops:
  0.6 32.2 %sketch.1 = (f32[64,2048]{1,0:T(8,128)S(1)}, f32[16,1024]{1,0:T(8,128)S(1)}, f32[8,32]{1,0:T(8,128)S(1)}) custom-call(f32[2048,1024]{1,0:T(8,128)} %f_hbm.1, f32[64,1024]{1,0:T(8,128)} %bitcast.3, f32[128,2048]{1,0:T(8,128)} %a_hbm.1, f32[256,2048]{1,0:T(8,128)} %l_hbm.1, f32[256,1024]{1,0:T(8,128)} %q_hbm.1), custom_call_target="tpu_custom_call" | custom-call | tf_op jit(solution)/shard_map/sketch/pallas_call | solution.py:330
  32.8 0.8 %store.1 = (f32[64,2048]{1,0:T(8,128)}, f32[16,1024]{1,0:T(8,128)}, f32[8,32]{1,0:T(8,128)}) custom-call(f32[64,2048]{1,0:T(8,128)S(1)} %get-tuple-element.9.refs_0_, f32[16,1024]{1,0:T(8,128)S(1)} %get-tuple-element.10.refs_1_, f32[8,32]{1,0:T(8,128)S(1)} %get-tuple-element.11.refs_2_), custom_call_target="tpu_custom_call" | custom-call | tf_op jit(solution)/shard_map/store/pallas_call | solution.py:380
